TPU v7x, 32 devices: a whole 2x2x4 slice. The times are simulated.
32 devices in a mesh: groups: 2 (over y), seq: 4 (over x, core), head: 4 (over z).
Axes of the slice: x: 2, y: 2, z: 4, core: 2. Of those that a mesh axis runs over, the one named last changes fastest.
Arguments:
- query_rows: bfloat16 [8192, 16, 128], P(('groups', 'seq'), 'head'), parts along dimension 0, may hold values from -16 to 16
- key_rows: bfloat16 [8192, 16, 128], P(('groups', 'seq'), 'head'), parts along dimension 0, may hold values from -10 to 10
- value_rows: bfloat16 [8192, 16, 128], P(('groups', 'seq'), 'head'), parts along dimension 0, may hold values from -6 to 6
- grad_rows: bfloat16 [8192, 16, 128], P(('groups', 'seq'), 'head'), parts along dimension 0, may hold values from -6 to 6
- clusters: int32 [16, 8192], P('head', ('groups', 'seq')), parts along dimension 1, may hold values from 0 to 3, as said below
- positions: int32 [8192], P(('groups', 'seq')), parts along dimension 0, may hold values from 0 to 4095, each once
Outputs:
- query_grad: bfloat16 [8192, 16, 128], P(('groups', 'seq'), 'head'), parts along dimension 0
- key_grad: bfloat16 [8192, 16, 128], P(('groups', 'seq'), 'head'), parts along dimension 0
- value_grad: bfloat16 [8192, 16, 128], P(('groups', 'seq'), 'head'), parts along dimension 0
- centroid_sums: float32 [16, 8, 128], P('head', ('groups', 'seq')), parts along dimension 1
There are 2 independent parts, one for each index of `groups`. A program takes and returns all parts, laid end to end along the dimension named above; each array names one. Nothing has to cross between parts.
Inputs may be any that keep to these rules, and one draw needn't show every extreme that they name: `clusters`: for each head every cluster holds exactly 1024 rows. Of the 1024 rows of one aligned block (the rows of one device along seq), the number whose cluster lies in one group g * 1 to g + 1 - 1 is 192, 256 or 320; in each head and block exactly one group receives 256 + 64 and exactly one 256 - 64. `positions`: each position occurs once.
All inputs are finite; a program needn't handle non-finite values.
Results may differ from a plain program's by a relative error of at most 0.012.
Values may be sent and summed in bfloat16 or wider, within the bound.
A program may use at most 128 MiB of HBM per device.

v0:
```python
import functools

import jax
import jax.numpy as jnp
from jax import lax
from jax.experimental import pallas as pl
from jax.experimental.pallas import tpu as pltpu
from jax.sharding import PartitionSpec as P

CL_DEV = 1


epsilon = 1e-06


def attend(query_block, key_block, value_block, grad_block, allowed):
    score_scale = query_block.shape[-1] ** (-0.5)
    scores = (
        lax.dot_general(
            query_block, key_block, (((1,), (1,)), ((), ())), preferred_element_type=jnp.float32
        )
        * score_scale
    )
    scores = jnp.where(allowed, scores, -1e30)
    highest = jnp.max(scores, axis=1, keepdims=True)
    exponent_terms = jnp.exp(scores - highest)
    weights = exponent_terms / jnp.sum(exponent_terms, axis=1, keepdims=True)
    weights_low = weights.astype(jnp.bfloat16)
    output = jnp.dot(weights_low, value_block, preferred_element_type=jnp.float32)
    row_delta = jnp.sum(grad_block.astype(jnp.float32) * output, axis=1, keepdims=True)
    prob_grad = lax.dot_general(
        grad_block, value_block, (((1,), (1,)), ((), ())), preferred_element_type=jnp.float32
    )
    score_grad = (weights * (prob_grad - row_delta)).astype(jnp.bfloat16)
    query_grad = (
        jnp.dot(score_grad, key_block, preferred_element_type=jnp.float32) * score_scale
    ).astype(jnp.bfloat16)
    key_grad = (
        lax.dot_general(
            score_grad, query_block, (((0,), (0,)), ((), ())), preferred_element_type=jnp.float32
        )
        * score_scale
    ).astype(jnp.bfloat16)
    value_grad = lax.dot_general(
        weights_low, grad_block, (((0,), (0,)), ((), ())), preferred_element_type=jnp.float32
    ).astype(jnp.bfloat16)
    return (query_grad, key_grad, value_grad)


def owner_head(rows_in, places_in, tags_in):
    head_width = rows_in.shape[1] // 4
    filled = tags_in > 0
    allowed = (
        (places_in[None, :] <= places_in[:, None])
        & (tags_in[None, :] == tags_in[:, None])
        & filled[None, :]
    )
    key_block = rows_in[:, head_width : 2 * head_width]
    grad_parts = attend(
        rows_in[:, :head_width],
        key_block,
        rows_in[:, 2 * head_width : 3 * head_width],
        rows_in[:, 3 * head_width :],
        allowed,
    )
    joined = jnp.concatenate(grad_parts, axis=1)
    centroid_rows = None
    key_float = key_block.astype(jnp.float32)
    unit_keys = key_float * lax.rsqrt(
        jnp.sum(key_float * key_float, axis=1, keepdims=True) + epsilon
    )
    tag_hits = (tags_in[:, None] == jnp.arange(1, CL_DEV + 1, dtype=jnp.int32)[None, :]).astype(
        jnp.float32
    )
    centroid_rows = lax.dot_general(
        tag_hits,
        unit_keys,
        (((0,), (0,)), ((), ())),
        precision=lax.Precision.HIGHEST,
        preferred_element_type=jnp.float32,
    )
    return (joined, centroid_rows)


def per_device(query_rows, key_rows, value_rows, grad_rows, clusters, positions):
    tok_count = query_rows.shape[0]
    head_width = query_rows.shape[2]
    sources = lax.axis_size("seq")
    peer_share = tok_count // sources
    capacity = peer_share + peer_share // 4
    total_slots = sources * capacity
    owner_of = clusters // CL_DEV
    local_tag = clusters % CL_DEV + 1
    owner_hits = (
        owner_of[:, :, None] == jnp.arange(sources, dtype=jnp.int32)[None, None, :]
    ).astype(jnp.int32)
    arrival = jnp.sum(jnp.cumsum(owner_hits, axis=1) * owner_hits, axis=2) - 1
    send_slot = owner_of * capacity + arrival
    slot_hits = send_slot[:, None, :] == jnp.arange(total_slots, dtype=jnp.int32)[None, :, None]
    slot_table = slot_hits.astype(jnp.bfloat16)
    payload = jnp.concatenate([query_rows, key_rows, value_rows, grad_rows], axis=2)
    send_rows = jnp.einsum(
        "hst,thd->hsd", slot_table, payload, preferred_element_type=jnp.float32
    ).astype(jnp.bfloat16)
    send_place = jnp.sum(jnp.where(slot_hits, positions[None, None, :], 0), axis=2)
    send_tag = jnp.sum(jnp.where(slot_hits, local_tag[:, None, :], 0), axis=2)
    centroid_parts = None
    rows_in = lax.all_to_all(send_rows, "seq", split_axis=1, concat_axis=1, tiled=True)
    places_in = lax.all_to_all(send_place, "seq", split_axis=1, concat_axis=1, tiled=True)
    tags_in = lax.all_to_all(send_tag, "seq", split_axis=1, concat_axis=1, tiled=True)
    grad_list = []
    centroid_list = []
    for head_at in range(rows_in.shape[0]):
        slot_grads, centroid_rows = owner_head(
            rows_in[head_at], places_in[head_at], tags_in[head_at]
        )
        grad_list.append(slot_grads)
        centroid_list.append(centroid_rows)
    stacked_grads = jnp.stack(grad_list, axis=0)
    stacked_grads, centroid_parts = (stacked_grads, jnp.stack(centroid_list, axis=0))
    returned = lax.all_to_all(stacked_grads, "seq", split_axis=1, concat_axis=1, tiled=True)
    home_rows = jnp.einsum(
        "hst,hsd->thd", slot_table, returned, preferred_element_type=jnp.float32
    ).astype(jnp.bfloat16)
    query_grad = home_rows[:, :, :head_width]
    key_grad = home_rows[:, :, head_width : 2 * head_width]
    value_grad = home_rows[:, :, 2 * head_width :]
    return (query_grad, key_grad, value_grad, centroid_parts)


def span_of(source, sources, total, low, high):
    first = max(source * low, total - (sources - source) * high)
    last = min((source + 1) * high, total - (sources - 1 - source) * low)
    return first, last


def exchange_kernel(
    sources,
    spans,
    meta_hbm,
    query_hbm,
    key_hbm,
    grad_hbm,
    value_hbm,
    dquery_hbm,
    dkey_hbm,
    dvalue_hbm,
    centroid_hbm,
    meta_in,
    pair_in,
    grad_in,
    value_in,
    pair_rows,
    grad_rows,
    value_rows,
    place_col,
    place_row,
    key_lines,
    key_cols,
    weights,
    score_low,
    dvalue_rows,
    dquery_rows,
    dkey_rows,
    stacked,
    centroid_out,
    send_sem,
    recv_sem,
    local_sem,
    *tables,
):
    pick = tables[:sources]
    unpick = tables[sources:]
    tokens = pair_in.shape[1]
    width = grad_in.shape[2]
    clusters = pair_rows.shape[0]
    rows = pair_rows.shape[1]
    scale = width ** (-0.5)
    me = lax.axis_index("seq")
    order = [sources // 2] + [d for d in range(1, sources) if d != sources // 2]

    def peer(d):
        return lax.rem(me + d, sources)

    def remote(array, d, src, dst):
        return pltpu.make_async_remote_copy(
            src_ref=src,
            dst_ref=dst,
            send_sem=send_sem.at[array, d - 1],
            recv_sem=recv_sem.at[array, d - 1],
            device_id={"seq": peer(d)},
            device_id_type=pl.DeviceIdType.MESH,
        )

    def exchange(array, src_at, dst):
        copies = [remote(array, d, src_at(peer(d)), dst) for d in order]
        own = pltpu.make_async_copy(src_at(me), dst, local_sem.at[array])
        for copy in copies:
            copy.start()
        own.start()
        return copies, own

    def arrive(started):
        copies, own = started
        own.wait()
        for copy in copies:
            copy.wait_recv()

    barrier = pltpu.get_barrier_semaphore()
    for d in range(1, sources):
        pl.semaphore_signal(
            barrier, inc=1, device_id={"seq": peer(d)}, device_id_type=pl.DeviceIdType.MESH
        )
    pl.semaphore_wait(barrier, sources - 1)

    meta_go = exchange(0, lambda to: meta_hbm.at[to], meta_in.at[me])
    key_go = exchange(2, lambda to: key_hbm.at[to], pair_in.at[me, :, width:])
    query_go = exchange(1, lambda to: query_hbm.at[to], pair_in.at[me, :, :width])

    tri_rows = tokens // 8

    @pl.loop(0, 8)
    def _(step):
        base = pl.multiple_of(step * tri_rows, tri_rows)
        before = lax.broadcasted_iota(jnp.int32, (tri_rows, tokens), 0) + base
        after = lax.broadcasted_iota(jnp.int32, (tri_rows, tokens), 1)
        score_low[pl.ds(base, tri_rows), :] = jnp.where(before < after, 1.0, 0.0).astype(
            jnp.bfloat16
        )

    arrive(meta_go)
    line = lax.broadcasted_iota(jnp.int32, (8, tokens), 0)
    line_float = line.astype(jnp.float32)
    base_count = jnp.zeros((8, 1), jnp.float32)
    lines = jnp.zeros((8, tokens), jnp.float32)
    for b in range(sources):
        first, last = spans[b]
        cluster = meta_in[b, 0:1, :]
        hits = jnp.where(cluster == line_float, 1.0, 0.0)
        rank = jnp.dot(
            hits.astype(jnp.bfloat16), score_low[...], preferred_element_type=jnp.float32
        )
        target = jnp.sum(hits * (rank + base_count), axis=0, keepdims=True)
        base_count = base_count + jnp.sum(hits, axis=1, keepdims=True)
        slot = cluster * float(last - first) + target - float(first)
        lines = jnp.where(line == b, slot, lines)
    key_lines[...] = lines
    key_cols[...] = jnp.transpose(lines)

    for b in range(sources):
        first, last = spans[b]
        many = clusters * (last - first)

        @pl.loop(0, many // 64)
        def _(step, b=b):
            base = pl.multiple_of(step * 64, 64)
            at = (lax.broadcasted_iota(jnp.int32, (64, tokens), 0) + base).astype(jnp.float32)
            pick[b][pl.ds(base, 64), :] = jnp.where(
                at == key_lines[b : b + 1, :], 1.0, 0.0
            ).astype(jnp.bfloat16)

        @pl.loop(0, tokens // 64)
        def _(step, b=b, many=many):
            base = pl.multiple_of(step * 64, 64)
            at = lax.broadcasted_iota(jnp.int32, (64, many), 1).astype(jnp.float32)
            unpick[b][pl.ds(base, 64), :] = jnp.where(
                at == key_cols[pl.ds(base, 64), b : b + 1], 1.0, 0.0
            ).astype(jnp.bfloat16)

    def gather(block_at, out, lanes=slice(None)):
        for b in range(sources):
            first, last = spans[b]
            size = last - first
            shared = spans[b - 1][1] - first if b > 0 else 0
            block = block_at(b)

            together = 2 if clusters % 2 == 0 else 1

            @pl.loop(0, clusters // together)
            def _(step, b=b, first=first, last=last, size=size, shared=shared, block=block):
                base = pl.multiple_of(step * together * size, 64)
                found = jnp.dot(
                    pick[b][pl.ds(base, together * size), :],
                    block,
                    preferred_element_type=jnp.float32,
                )
                for at in range(together):
                    c = step * together + at
                    part = found[at * size : (at + 1) * size]
                    if shared > 0:
                        out[c, first : first + shared, lanes] = (
                            out[c, first : first + shared, lanes].astype(jnp.float32)
                            + part[:shared]
                        ).astype(out.dtype)
                    out[c, first + shared : last, lanes] = part[shared:].astype(out.dtype)

    gather(lambda b: jnp.transpose(meta_in[b]).astype(jnp.bfloat16), place_col)

    @pl.loop(0, clusters)
    def _(c):
        place_row[c] = jnp.transpose(place_col[c])

    arrive(key_go)
    grad_go = exchange(3, lambda to: grad_hbm.at[to], grad_in.at[me])
    gather(lambda b: pair_in[b, :, width:], pair_rows, slice(width, 2 * width))

    @pl.loop(0, clusters)
    def _(c):
        keys = pair_rows[c, :, width:].astype(jnp.float32)
        unit = keys * lax.rsqrt(jnp.sum(keys * keys, axis=1, keepdims=True) + epsilon)
        centroid_out[c] = jnp.broadcast_to(jnp.sum(unit, axis=0, keepdims=True), (8, width))

    centroid_go = exchange(5, lambda to: centroid_out.at[to], centroid_hbm.at[me])

    arrive(query_go)
    value_go = exchange(4, lambda to: value_hbm.at[to], value_in.at[me])
    gather(lambda b: pair_in[b, :, :width], pair_rows, slice(0, width))

    tile = min(256, rows)
    tiles = rows // tile

    @pl.loop(0, clusters * tiles)
    def _(step):
        c = step // tiles
        base = pl.multiple_of((step % tiles) * tile, tile)
        scores = lax.dot_general(
            pair_rows[c, :, width:],
            pair_rows[c, pl.ds(base, tile), :width],
            (((1,), (1,)), ((), ())),
            preferred_element_type=jnp.float32,
        )
        place_u = place_col[c, :, 1:2] * 64.0 + place_col[c, :, 2:3]
        place_t = (
            place_row[c, 1:2, pl.ds(base, tile)] * 64.0 + place_row[c, 2:3, pl.ds(base, tile)]
        )
        scores = jnp.where(place_u <= place_t, scores, -1e30)
        highest = jnp.max(scores, axis=0, keepdims=True)
        terms = jnp.exp2((scores - highest) * (scale * 1.4426950408889634))
        inverse = 1.0 / jnp.sum(terms, axis=0, keepdims=True)
        weights[c, :, pl.ds(base, tile)] = terms * inverse

    def go_home(source, home, lanes, array, target):
        half = sources // 2
        turn = tokens // 2

        @pl.loop(0, sources)
        def _(step):
            late = step // half
            d = (half + step) * (1 - late) + (sources - 1 - step) * late
            to = peer(d)
            for b in range(sources):

                @pl.when(to == b)
                def _(b=b):
                    first, last = spans[b]
                    size = last - first
                    for c in range(clusters):
                        stacked[c * size : (c + 1) * size, :] = source[c, first:last, :]

                    @pl.loop(0, tokens // turn)
                    def _(part):
                        base = pl.multiple_of(part * turn, turn)
                        home[b, pl.ds(base, turn), lanes] = jnp.dot(
                            unpick[b][pl.ds(base, turn), :],
                            stacked[: clusters * size, :],
                            preferred_element_type=jnp.float32,
                        ).astype(jnp.bfloat16)

            @pl.when(step < sources - 1)
            def _():
                remote(array, d, home.at[to, :, lanes], target.at[me]).start()

        own = pltpu.make_async_copy(home.at[me, :, lanes], target.at[me], local_sem.at[array])
        own.start()
        return [
            remote(array, d, home.at[peer(d), :, lanes], target.at[me])
            for d in range(1, sources)
        ] + [own]

    arrive(grad_go)
    gather(lambda b: grad_in[b], grad_rows)

    @pl.loop(0, clusters)
    def _(c):
        dvalue_rows[c] = jnp.dot(
            weights[c].astype(jnp.bfloat16), grad_rows[c], preferred_element_type=jnp.float32
        ).astype(jnp.bfloat16)

    home_go = go_home(dvalue_rows, grad_in, slice(None), 6, dvalue_hbm)

    arrive(value_go)
    gather(lambda b: value_in[b], value_rows)

    @pl.loop(0, clusters)
    def _(c):
        keys_turned = jnp.transpose(pair_rows[c, :, width:])

        @pl.loop(0, tiles)
        def _(step):
            base = pl.multiple_of(step * tile, tile)
            prob = lax.dot_general(
                value_rows[c],
                grad_rows[c, pl.ds(base, tile), :],
                (((1,), (1,)), ((), ())),
                preferred_element_type=jnp.float32,
            )
            part = weights[c, :, pl.ds(base, tile)]
            part_low = part.astype(jnp.bfloat16).astype(jnp.float32)
            delta = jnp.sum(part_low * prob, axis=0, keepdims=True)
            score_grad = (part * (prob - delta)).astype(jnp.bfloat16)
            score_low[:, pl.ds(base, tile)] = score_grad
            turned = jnp.dot(keys_turned, score_grad, preferred_element_type=jnp.float32)
            dquery_rows[c, pl.ds(base, tile), :] = jnp.transpose(turned * scale).astype(
                jnp.bfloat16
            )

        dkey_rows[c] = (
            jnp.dot(
                score_low[...], pair_rows[c, :, :width], preferred_element_type=jnp.float32
            )
            * scale
        ).astype(jnp.bfloat16)

    home_go += go_home(dquery_rows, pair_in, slice(0, width), 7, dquery_hbm)
    home_go += go_home(dkey_rows, pair_in, slice(width, 2 * width), 8, dkey_hbm)

    arrive(centroid_go)
    for copies, _own in (meta_go, query_go, key_go, grad_go, value_go, centroid_go):
        for copy in copies:
            copy.wait_send()
    for copy in home_go:
        copy.wait()


def per_device_heads(query_rows, key_rows, value_rows, grad_rows, clusters, positions):
    tokens, heads, width = query_rows.shape
    sources = lax.axis_size("seq")
    total = tokens
    share = tokens // sources
    spans = [
        span_of(b, sources, total, share - share // 4, share + share // 4) for b in range(sources)
    ]
    places = jnp.broadcast_to(positions[None, :], (heads, tokens))
    blank = jnp.zeros_like(places)
    meta = jnp.stack(
        [clusters, places // 64, places % 64, blank, blank, blank, blank, blank], axis=1
    ).astype(jnp.float32)
    by_head = [
        jnp.transpose(rows, (1, 0, 2)) for rows in (query_rows, key_rows, grad_rows, value_rows)
    ]
    anywhere = pl.BlockSpec(memory_space=pl.ANY)
    rows_shape = jax.ShapeDtypeStruct((heads, tokens, width), jnp.bfloat16)
    low = jnp.bfloat16
    full = jnp.float32
    sizes = [sources * (last - first) for first, last in spans]
    scratch = [
        pltpu.VMEM((sources, 8, tokens), full),
        pltpu.VMEM((sources, tokens, 2 * width), low),
        pltpu.VMEM((sources, tokens, width), low),
        pltpu.VMEM((sources, tokens, width), low),
        pltpu.VMEM((sources, total, 2 * width), low),
        pltpu.VMEM((sources, total, width), low),
        pltpu.VMEM((sources, total, width), low),
        pltpu.VMEM((sources, total, 8), full),
        pltpu.VMEM((sources, 8, total), full),
        pltpu.VMEM((8, tokens), full),
        pltpu.VMEM((tokens, 8), full),
        pltpu.VMEM((sources, total, total), full),
        pltpu.VMEM((total, total), low),
        pltpu.VMEM((sources, total, width), low),
        pltpu.VMEM((sources, total, width), low),
        pltpu.VMEM((sources, total, width), low),
        pltpu.VMEM((max(sizes), width), low),
        pltpu.VMEM((sources, 8, width), full),
        pltpu.SemaphoreType.DMA((9, sources - 1)),
        pltpu.SemaphoreType.DMA((9, sources - 1)),
        pltpu.SemaphoreType.DMA((9,)),
    ]
    scratch += [pltpu.VMEM((size, tokens), low) for size in sizes]
    scratch += [pltpu.VMEM((tokens, size), low) for size in sizes]
    outs = pl.pallas_call(
        functools.partial(exchange_kernel, sources, spans),
        out_shape=(
            rows_shape,
            rows_shape,
            rows_shape,
            jax.ShapeDtypeStruct((heads, 8, width), full),
        ),
        in_specs=[anywhere] * 5,
        out_specs=(anywhere,) * 4,
        scratch_shapes=scratch,
        compiler_params=pltpu.CompilerParams(
            collective_id=0, has_side_effects=True, vmem_limit_bytes=62 * 1024 * 1024
        ),
    )(meta, *by_head)
    dquery, dkey, dvalue = [jnp.transpose(rows, (1, 0, 2)) for rows in outs[:3]]
    return dquery, dkey, dvalue, outs[3][:, 0:1, :]


def solution(mesh):
    sources = mesh.shape["seq"]

    def body(query_rows, *others):
        if query_rows.shape[1] == sources and sources % 2 == 0 and CL_DEV == 1:
            return per_device_heads(query_rows, *others)
        return per_device(query_rows, *others)

    return jax.shard_map(
        body,
        mesh=mesh,
        in_specs=(
            P(("groups", "seq"), "head", None),
            P(("groups", "seq"), "head", None),
            P(("groups", "seq"), "head", None),
            P(("groups", "seq"), "head", None),
            P("head", ("groups", "seq")),
            P(("groups", "seq")),
        ),
        out_specs=(
            P(("groups", "seq"), "head", None),
            P(("groups", "seq"), "head", None),
            P(("groups", "seq"), "head", None),
            P("head", ("groups", "seq"), None),
        ),
        check_vma=False,
    )
```

profile of v0, /device:TPU:0, one launch (start us, length us, event | category | flops | bytes accessed | tf_op | source)
XLA Modules:
  0.0 123.3 jit_solution(3656131704766227169)
XLA Ops:
  0.6 0.7 compare_and_fusion
  1.3 0.0 copy-start.4
  1.3 0.7 stack.11
  2.1 0.0 copy-done.4
  2.2 0.1 stack.13
  2.3 0.7 convert_element_type.3.meta_hbm
  3.0 0.0 copy-start.2
  3.0 0.0 copy-start.3
  3.0 3.3 %copy_bitcast_fusion.2 = (bf16[4,1024,128]{2,1,0:T(8,128)(2,1)}, bf16[4,1024,128]{2,1,0:T(8,128)(2,1)}) fusion(bf16[1024,4,128]{2,1,0:T(4,128)(2,1)} %param.7, bf16[1024,4,128]{2,1,0:T(4,128)(2,1)} %param.6), kind=kLoop, calls=%fused_computation.2 | loop fusion | bytes 4194304 | tf_op jit(solution)/shard_map/transpose | solution.py:449
  6.2 0.0 copy-done.2
  6.2 0.0 copy-done.3
  6.2 1.6 %copy_bitcast_fusion = (bf16[4,1024,128]{2,1,0:T(8,128)(2,1)}, bf16[4,1024,128]{2,1,0:T(8,128)(2,1)}) fusion(bf16[1024,4,128]{2,1,0:T(4,128)(2,1)S(1)} %copy-done.2, bf16[1024,4,128]{2,1,0:T(4,128)(2,1)S(1)} %copy-done.3), kind=kLoop, calls=%fused_computation | loop fusion | bytes 4194304 | tf_op jit(solution)/shard_map/transpose | solution.py:449
  7.8 107.5 %shard_map.93 = (bf16[4,1024,128]{2,1,0:T(8,128)(2,1)}, bf16[4,1024,128]{2,1,0:T(8,128)(2,1)}, bf16[4,1024,128]{2,1,0:T(8,128)(2,1)}, f32[4,8,128]{2,1,0:T(8,128)}) custom-call(f32[4,8,1024]{2,1,0:T(8,128)} %convert_element_type.3.meta_hbm, bf16[4,1024,128]{2,1,0:T(8,128)(2,1)} %get-tuple-element.27.query_hbm, ...), custom_call_target="tpu_custom_call" | custom-call | tf_op jit(solution)/shard_map/pallas_call | solution.py:481
  115.3 0.0 copy-start.1
  115.3 3.1 %copy.14 = bf16[1024,4,128]{2,1,0:T(4,128)(2,1)} copy(bf16[1024,4,128]{2,0,1:T(8,128)(2,1)} %bitcast.13) | data formatting | bytes 2097152
  118.4 0.0 copy-done.1
  118.4 0.0 copy-start
  118.4 1.8 %copy.15 = bf16[1024,4,128]{2,1,0:T(4,128)(2,1)} copy(bf16[1024,4,128]{2,0,1:T(8,128)(2,1)S(1)} %bitcast.12) | data formatting | bytes 2097152
  120.2 1.3 %slice.3 = f32[4,1,128]{2,1,0:T(1,128)} slice(f32[4,8,128]{2,1,0:T(8,128)} %get-tuple-element.11), slice={[0:4], [0:1], [0:128]} | slice | bytes 4096 | tf_op jit(solution)/shard_map/slice | solution.py:497
  121.5 0.0 copy-done
  121.5 1.8 %copy.16 = bf16[1024,4,128]{2,1,0:T(4,128)(2,1)} copy(bf16[1024,4,128]{2,0,1:T(8,128)(2,1)S(1)} %bitcast.11) | data formatting | bytes 2097152
  (4 shorter events, 0.1 us)
Async XLA Ops:
  1.3 0.7 copy-start.4
  3.0 3.3 %copy-start.2 = (bf16[1024,4,128]{2,1,0:T(4,128)(2,1)S(1)}, bf16[1024,4,128]{2,1,0:T(4,128)(2,1)}, u32[]{:S(2)}) copy-start(bf16[1024,4,128]{2,1,0:T(4,128)(2,1)} %param.8) | copy-start | bytes 3145732
  3.0 3.3 %copy-start.3 = (bf16[1024,4,128]{2,1,0:T(4,128)(2,1)S(1)}, bf16[1024,4,128]{2,1,0:T(4,128)(2,1)}, u32[]{:S(2)}) copy-start(bf16[1024,4,128]{2,1,0:T(4,128)(2,1)} %param.9) | copy-start | bytes 3145732
  115.3 3.1 %copy-start.1 = (bf16[4,1024,128]{2,1,0:T(8,128)(2,1)S(1)}, bf16[4,1024,128]{2,1,0:T(8,128)(2,1)}, u32[]{:S(2)}) copy-start(bf16[4,1024,128]{2,1,0:T(8,128)(2,1)} %get-tuple-element.9) | copy-start | bytes 3145732
  118.4 3.1 %copy-start = (bf16[4,1024,128]{2,1,0:T(8,128)(2,1)S(1)}, bf16[4,1024,128]{2,1,0:T(8,128)(2,1)}, u32[]{:S(2)}) copy-start(bf16[4,1024,128]{2,1,0:T(8,128)(2,1)} %get-tuple-element.10) | copy-start | bytes 3145732
where the time goes:
time: 124 us; the launch traced here: 123 us
  Pallas kernels  107 us (86%)
  local copies, waits for them, and re-layouts  13.7 us (11%)
  other arithmetic  1.39 us (1%)
    pallas_call x1, Pallas kernels, per_device_heads(): pl.pallas_call(functools.partial(exchange_kernel, sources, spans), out_sh...  107 us
    unnamed x13, local copies, waits for them, and re-layouts  6.67 us
    transpose x2, local copies, waits for them, and re-layouts, per_device_heads(): jnp.transpose(rows, (1, 0, 2))  4.87 us

commit v1 on v0

--- a/solution.py
+++ b/solution.py
@@ -267,14 +267,13 @@
                 at == key_cols[pl.ds(base, 64), b : b + 1], 1.0, 0.0
             ).astype(jnp.bfloat16)
 
-    def gather(block_at, out, lanes=slice(None)):
+    def gather(block_at, out, lanes=slice(None), together=2):
         for b in range(sources):
             first, last = spans[b]
             size = last - first
             shared = spans[b - 1][1] - first if b > 0 else 0
             block = block_at(b)
 
-            together = 2 if clusters % 2 == 0 else 1
 
             @pl.loop(0, clusters // together)
             def _(step, b=b, first=first, last=last, size=size, shared=shared, block=block):
@@ -341,7 +340,7 @@
 
     def go_home(source, home, lanes, array, target):
         half = sources // 2
-        turn = tokens // 2
+        turn = tokens
 
         @pl.loop(0, sources)
         def _(step):
@@ -378,7 +377,7 @@
         ] + [own]
 
     arrive(grad_go)
-    gather(lambda b: grad_in[b], grad_rows)
+    gather(lambda b: grad_in[b], grad_rows, together=clusters)
 
     @pl.loop(0, clusters)
     def _(c):
@@ -389,7 +388,7 @@
     home_go = go_home(dvalue_rows, grad_in, slice(None), 6, dvalue_hbm)
 
     arrive(value_go)
-    gather(lambda b: value_in[b], value_rows)
+    gather(lambda b: value_in[b], value_rows, together=clusters)
 
     @pl.loop(0, clusters)
     def _(c):

time: 124 us -> 120 us (0.968)
  Pallas kernels: 107 us -> 104 us
    pallas_call x1, Pallas kernels: 107 us -> 104 us  [per_device_heads(): pl.pallas_call(functools.partial(exchange_kernel, sources, spans), out_sh...]
where the time goes in v1:
time: 120 us
  Pallas kernels  104 us (87%)
  local copies, waits for them, and re-layouts  13.7 us (11%)
  other arithmetic  1.39 us (1%)
    pallas_call x1, Pallas kernels, per_device_heads(): pl.pallas_call(functools.partial(exchange_kernel, sources, spans), out_sh...  104 us
    unnamed x13, local copies, waits for them, and re-layouts  6.67 us
    transpose x2, local copies, waits for them, and re-layouts, per_device_heads(): jnp.transpose(rows, (1, 0, 2))  4.87 us

profile of v1, /device:TPU:0, one launch (start us, length us, event | category | flops | bytes accessed | tf_op | source)
XLA Modules:
  0.0 120.2 jit_solution(8246552272837428286)
XLA Ops:
  0.6 0.7 compare_and_fusion
  1.3 0.0 copy-start.4
  1.3 0.7 stack.11
  2.1 0.0 copy-done.4
  2.2 0.1 stack.13
  2.3 0.7 convert_element_type.3.meta_hbm
  3.0 0.0 copy-start.2
  3.0 0.0 copy-start.3
  3.0 3.3 %copy_bitcast_fusion.2 = (bf16[4,1024,128]{2,1,0:T(8,128)(2,1)}, bf16[4,1024,128]{2,1,0:T(8,128)(2,1)}) fusion(bf16[1024,4,128]{2,1,0:T(4,128)(2,1)} %param.7, bf16[1024,4,128]{2,1,0:T(4,128)(2,1)} %param.6), kind=kLoop, calls=%fused_computation.2 | loop fusion | bytes 4194304 | tf_op jit(solution)/shard_map/transpose | solution.py:448
  6.2 0.0 copy-done.2
  6.2 0.0 copy-done.3
  6.2 1.6 %copy_bitcast_fusion = (bf16[4,1024,128]{2,1,0:T(8,128)(2,1)}, bf16[4,1024,128]{2,1,0:T(8,128)(2,1)}) fusion(bf16[1024,4,128]{2,1,0:T(4,128)(2,1)S(1)} %copy-done.2, bf16[1024,4,128]{2,1,0:T(4,128)(2,1)S(1)} %copy-done.3), kind=kLoop, calls=%fused_computation | loop fusion | bytes 4194304 | tf_op jit(solution)/shard_map/transpose | solution.py:448
  7.8 104.3 %shard_map.93 = (bf16[4,1024,128]{2,1,0:T(8,128)(2,1)}, bf16[4,1024,128]{2,1,0:T(8,128)(2,1)}, bf16[4,1024,128]{2,1,0:T(8,128)(2,1)}, f32[4,8,128]{2,1,0:T(8,128)}) custom-call(f32[4,8,1024]{2,1,0:T(8,128)} %convert_element_type.3.meta_hbm, bf16[4,1024,128]{2,1,0:T(8,128)(2,1)} %get-tuple-element.27.query_hbm, ...), custom_call_target="tpu_custom_call" | custom-call | tf_op jit(solution)/shard_map/pallas_call | solution.py:480
  112.2 0.0 copy-start.1
  112.2 3.1 %copy.14 = bf16[1024,4,128]{2,1,0:T(4,128)(2,1)} copy(bf16[1024,4,128]{2,0,1:T(8,128)(2,1)} %bitcast.13) | data formatting | bytes 2097152
  115.3 0.0 copy-done.1
  115.3 0.0 copy-start
  115.3 1.8 %copy.15 = bf16[1024,4,128]{2,1,0:T(4,128)(2,1)} copy(bf16[1024,4,128]{2,0,1:T(8,128)(2,1)S(1)} %bitcast.12) | data formatting | bytes 2097152
  117.1 1.3 %slice.3 = f32[4,1,128]{2,1,0:T(1,128)} slice(f32[4,8,128]{2,1,0:T(8,128)} %get-tuple-element.11), slice={[0:4], [0:1], [0:128]} | slice | bytes 4096 | tf_op jit(solution)/shard_map/slice | solution.py:496
  118.4 0.0 copy-done
  118.4 1.8 %copy.16 = bf16[1024,4,128]{2,1,0:T(4,128)(2,1)} copy(bf16[1024,4,128]{2,0,1:T(8,128)(2,1)S(1)} %bitcast.11) | data formatting | bytes 2097152
  (4 shorter events, 0.1 us)
Async XLA Ops:
  1.3 0.7 copy-start.4
  3.0 3.3 %copy-start.2 = (bf16[1024,4,128]{2,1,0:T(4,128)(2,1)S(1)}, bf16[1024,4,128]{2,1,0:T(4,128)(2,1)}, u32[]{:S(2)}) copy-start(bf16[1024,4,128]{2,1,0:T(4,128)(2,1)} %param.8) | copy-start | bytes 3145732
  3.0 3.3 %copy-start.3 = (bf16[1024,4,128]{2,1,0:T(4,128)(2,1)S(1)}, bf16[1024,4,128]{2,1,0:T(4,128)(2,1)}, u32[]{:S(2)}) copy-start(bf16[1024,4,128]{2,1,0:T(4,128)(2,1)} %param.9) | copy-start | bytes 3145732
  112.2 3.1 %copy-start.1 = (bf16[4,1024,128]{2,1,0:T(8,128)(2,1)S(1)}, bf16[4,1024,128]{2,1,0:T(8,128)(2,1)}, u32[]{:S(2)}) copy-start(bf16[4,1024,128]{2,1,0:T(8,128)(2,1)} %get-tuple-element.9) | copy-start | bytes 3145732
  115.3 3.1 %copy-start = (bf16[4,1024,128]{2,1,0:T(8,128)(2,1)S(1)}, bf16[4,1024,128]{2,1,0:T(8,128)(2,1)}, u32[]{:S(2)}) copy-start(bf16[4,1024,128]{2,1,0:T(8,128)(2,1)} %get-tuple-element.10) | copy-start | bytes 3145732
